TPU v7x, 32 devices: a whole 2x2x4 slice. The times are simulated.
32 devices in a mesh: dp: 4 (over y, x), expert: 8 (over z, core).
Axes of the slice: x: 2, y: 2, z: 4, core: 2. Of those that a mesh axis runs over, the one named last changes fastest.
Arguments:
- tokens: bfloat16 [4096, 4096], P(('dp', 'expert')), may hold values from -6 to 6
- out_grad: bfloat16 [4096, 4096], P(('dp', 'expert')), may hold values from -0.75 to 0.75
- routes: int32 [4096, 1], P(('dp', 'expert')), may hold values from 0 to 7; in each aligned block of 128 rows (0 to 127, 128 to 255, ...) at most 24 rows name the same one
- gate_probs: bfloat16 [4096, 1], P(('dp', 'expert')), may hold values from 0.049804688 to 1
- w_gate: bfloat16 [8, 4096, 768], P('expert', None, 'dp'), may hold values from -0.09375 to 0.09375
- w_up: bfloat16 [8, 4096, 768], P('expert', None, 'dp'), may hold values from -0.09375 to 0.09375
- w_down: bfloat16 [8, 768, 4096], P('expert', 'dp'), may hold values from -0.21875 to 0.21875
Outputs:
- grad_tokens: bfloat16 [4096, 4096], P(('dp', 'expert'))
- grad_probs: bfloat16 [4096, 1], P(('dp', 'expert'))
- grad_w_gate: bfloat16 [8, 4096, 768], P('expert', None, 'dp')
- grad_w_up: bfloat16 [8, 4096, 768], P('expert', None, 'dp')
- grad_w_down: bfloat16 [8, 768, 4096], P('expert', 'dp')
Inputs may be any that keep to these rules, and one draw needn't show every extreme that they name: `routes`: the experts of one token are different. Among the 128 tokens of one device no expert is named more than 24 times, a bound that some block reaches.
All inputs are finite; a program needn't handle non-finite values.
Results may differ from a plain program's by a relative error of at most 0.018.
Values may be sent and summed in bfloat16 or wider, within the bound.
A program may use at most 128 MiB of HBM per device.

v0:
```python
import jax
import jax.numpy as jnp
from jax import lax
from jax.sharding import PartitionSpec as P


def body(tokens, out_grad, routes, gate_probs, w_gate, w_up, w_down):
    expert_count = lax.axis_size("expert")
    tok_count, width = tokens.shape
    top_count = routes.shape[1]
    capacity = 3 * tok_count * top_count // (2 * expert_count)
    slot_total = expert_count * capacity
    flat_routes = routes.reshape(-1)
    one_hot = (flat_routes[:, None] == jnp.arange(expert_count, dtype=jnp.int32)[None, :]).astype(
        jnp.int32
    )
    earlier = jnp.cumsum(one_hot, axis=0) - one_hot
    slot_index = jnp.sum(earlier * one_hot, axis=1)
    destination = flat_routes * capacity + slot_index
    placing = (jnp.arange(slot_total, dtype=jnp.int32)[:, None] == destination[None, :]).astype(
        jnp.bfloat16
    )
    collect = jnp.sum(placing.reshape(slot_total, tok_count, top_count), axis=2)
    sent_in = (
        jnp.dot(collect, tokens, preferred_element_type=jnp.float32)
        .astype(jnp.bfloat16)
        .reshape(expert_count, capacity, width)
    )
    sent_dy = (
        jnp.dot(collect, out_grad, preferred_element_type=jnp.float32)
        .astype(jnp.bfloat16)
        .reshape(expert_count, capacity, width)
    )
    sent_prob = (
        jnp.dot(placing, gate_probs.reshape(-1), preferred_element_type=jnp.float32)
        .astype(jnp.bfloat16)
        .reshape(expert_count, capacity)
    )
    recv_in, recv_dy, recv_prob = (
        lax.all_to_all(sent_in, "expert", split_axis=0, concat_axis=0, tiled=True),
        lax.all_to_all(sent_dy, "expert", split_axis=0, concat_axis=0, tiled=True),
        lax.all_to_all(sent_prob, "expert", split_axis=0, concat_axis=0, tiled=True),
    )
    all_in, all_dy, all_prob = (
        lax.all_gather(recv_in, "dp", axis=0, tiled=True),
        lax.all_gather(recv_dy, "dp", axis=0, tiled=True),
        lax.all_gather(recv_prob, "dp", axis=0, tiled=True),
    )
    row_total = all_in.shape[0] * capacity
    rows_in = all_in.reshape(row_total, width)
    rows_dy = all_dy.reshape(row_total, width)
    rows_prob = all_prob.reshape(row_total)
    gate_w = w_gate[0]
    up_w = w_up[0]
    down_w = w_down[0]
    contract_last = (((1,), (1,)), ((), ()))
    contract_first = (((0,), (0,)), ((), ()))
    gate_pre = jnp.dot(rows_in, gate_w, preferred_element_type=jnp.float32)
    up_pre = jnp.dot(rows_in, up_w, preferred_element_type=jnp.float32)
    sigmoid_gate = jax.nn.sigmoid(gate_pre)
    active = gate_pre * sigmoid_gate
    hidden = (active * up_pre).astype(jnp.bfloat16)
    back_raw = lax.dot_general(rows_dy, down_w, contract_last, preferred_element_type=jnp.float32)
    weight_col = rows_prob.astype(jnp.float32)[:, None]
    scaled = (weight_col * rows_dy.astype(jnp.float32)).astype(jnp.bfloat16)
    grad_down = lax.dot_general(
        hidden, scaled, contract_first, preferred_element_type=jnp.float32
    ).astype(jnp.bfloat16)
    back_hidden = weight_col * back_raw
    grad_gate_pre = (
        back_hidden * up_pre * sigmoid_gate * (1.0 + gate_pre * (1.0 - sigmoid_gate))
    ).astype(jnp.bfloat16)
    grad_up_pre = (back_hidden * active).astype(jnp.bfloat16)
    grad_gate = lax.dot_general(
        rows_in, grad_gate_pre, contract_first, preferred_element_type=jnp.float32
    ).astype(jnp.bfloat16)
    grad_up = lax.dot_general(
        rows_in, grad_up_pre, contract_first, preferred_element_type=jnp.float32
    ).astype(jnp.bfloat16)
    row_part = lax.dot_general(
        grad_gate_pre, gate_w, contract_last, preferred_element_type=jnp.float32
    )
    row_part = row_part + lax.dot_general(
        grad_up_pre, up_w, contract_last, preferred_element_type=jnp.float32
    )
    own_rows = lax.psum_scatter(
        row_part.astype(jnp.bfloat16), "dp", scatter_dimension=0, tiled=True
    )
    outputs = jnp.dot(hidden, down_w, preferred_element_type=jnp.float32)
    own_out = lax.psum_scatter(
        outputs.astype(jnp.bfloat16), "dp", scatter_dimension=0, tiled=True
    ).astype(jnp.float32)
    own_dy = recv_dy.reshape(slot_total, width).astype(jnp.float32)
    scores = jnp.sum(own_out * own_dy, axis=1)
    back_rows, back_scores = (
        lax.all_to_all(
            own_rows.reshape(expert_count, capacity, width),
            "expert",
            split_axis=0,
            concat_axis=0,
            tiled=True,
        ),
        lax.all_to_all(
            scores.astype(jnp.bfloat16).reshape(expert_count, capacity),
            "expert",
            split_axis=0,
            concat_axis=0,
            tiled=True,
        ),
    )
    grad_tokens = lax.dot_general(
        collect,
        back_rows.reshape(slot_total, width),
        contract_first,
        preferred_element_type=jnp.float32,
    ).astype(jnp.bfloat16)
    grad_probs = (
        jnp.dot(back_scores.reshape(slot_total), placing, preferred_element_type=jnp.float32)
        .astype(jnp.bfloat16)
        .reshape(tok_count, top_count)
    )
    return (grad_tokens, grad_probs, grad_gate[None], grad_up[None], grad_down[None])


def solution(mesh):
    in_specs = (
        P(("dp", "expert"), None),
        P(("dp", "expert"), None),
        P(("dp", "expert"), None),
        P(("dp", "expert"), None),
        P("expert", None, "dp"),
        P("expert", None, "dp"),
        P("expert", "dp", None),
    )
    out_specs = (
        P(("dp", "expert"), None),
        P(("dp", "expert"), None),
        P("expert", None, "dp"),
        P("expert", None, "dp"),
        P("expert", "dp", None),
    )
    return jax.shard_map(body, mesh=mesh, in_specs=in_specs, out_specs=out_specs, check_vma=False)
```

profile of v0, /device:TPU:11, one launch (start us, length us, event | category | flops | bytes accessed | tf_op | source)
XLA Modules:
  0.0 399.4 jit_solution(270262075053408817)
XLA Ops:
  7.2 0.0 copy-start
  7.2 0.0 all-gather.6.cloned.1.call-start
  7.2 0.8 fusion.24
  8.1 0.2 reduce_window_sum.11
  8.3 0.8 select_reduce_fusion
  9.1 0.7 multiply_add_fusion
  9.8 0.0 copy-start.4
  9.8 1.9 convolution_convert_fusion.3
  11.6 40.2 %all_to_all.34 = bf16[8,24,4096]{2,1,0:T(8,128)(2,1)} all-to-all(bf16[8,24,4096]{2,1,0:T(8,128)(2,1)S(1)} %bitcast.65), channel_id=1, replica_groups=mesh['dp'=4,'expert'=8] {'expert'}, dimensions={0} | all-to-all | bytes 3145728 | tf_op jit(solution)/shard_map/all_to_all | solution.py:40
  51.9 0.0 all-gather.6.cloned.1.call-update
  51.9 0.0 copy-start.8
  51.9 0.0 all-gather.4.cloned.1.call-start
  52.0 0.0 copy-done.4
  52.0 0.6 convolution_convert_fusion.4
  52.5 41.0 %all_to_all.35 = bf16[8,24,4096]{2,1,0:T(8,128)(2,1)} all-to-all(bf16[8,24,4096]{2,1,0:T(8,128)(2,1)S(1)} %bitcast.66), channel_id=1, replica_groups=mesh['dp'=4,'expert'=8] {'expert'}, dimensions={0} | all-to-all | bytes 3145728 | tf_op jit(solution)/shard_map/all_to_all | solution.py:41
  93.5 0.0 all-gather.4.cloned.1.call-update
  93.5 0.0 reduce-scatter.5.cloned.1.call-start
  93.6 0.0 copy-done.8
  93.6 0.1 fusion.23
  93.8 0.1 all_to_all.28
  93.9 9.4 %all_to_all.36 = bf16[8,1,24]{2,1,0:T(2,128)(2,1)S(1)} all-to-all(bf16[8,1,24]{2,1,0:T(2,128)(2,1)S(1)} %all_to_all.28), channel_id=1, replica_groups=mesh['dp'=4,'expert'=8] {'expert'}, dimensions={0} | all-to-all | bytes 768 | tf_op jit(solution)/shard_map/all_to_all | solution.py:42
  103.2 6.7 %all-gather = bf16[32,1,24]{2,0,1:T(8,128)(2,1)S(1)} all-gather(bf16[8,1,24]{2,0,1:T(8,128)(2,1)S(1)} %copy.15), channel_id=2, replica_groups=mesh['dp'=4,'expert'=8] {'dp'}, dimensions={0}, use_global_device_ids=true | all-gather | bytes 1920 | tf_op jit(solution)/shard_map/all_gather | solution.py:47
  109.9 0.1 reshape.108
  110.0 13.4 %all-gather.6.cloned.1.call-done = bf16[32,24,4096]{2,1,0:T(8,128)(2,1)} async-done(((bf16[8,24,4096]{2,1,0:T(8,128)(2,1)}), bf16[32,24,4096]{2,1,0:T(8,128)(2,1)}) %all-gather.6.cloned.1.call-update) | async-done | bytes 6291472 | tf_op jit(solution)/shard_map/all_gather | solution.py:45
  123.4 0.0 copy-start.2
  123.4 6.4 %fusion.9 = f32[768,192]{0,1:T(8,128)} fusion(bf16[768,4096]{1,0:T(8,128)(2,1)} %bitcast.70, bf16[1,4096,192]{1,2,0:T(8,128)(2,1)} %param.11), kind=kOutput, calls=%fused_computation.18 | convolution fusion | flops 1207959552 | bytes 8454144 | tf_op jit(solution)/shard_map/dot_general | solution.py:58
  129.8 65.7 %all-gather.4.cloned.1.call-done = bf16[32,24,4096]{2,1,0:T(8,128)(2,1)} async-done(((bf16[8,24,4096]{2,1,0:T(8,128)(2,1)}), bf16[32,24,4096]{2,1,0:T(8,128)(2,1)}) %all-gather.4.cloned.1.call-update) | async-done | bytes 6291472 | tf_op jit(solution)/shard_map/all_gather | solution.py:46
  195.5 0.0 copy-done.2
  195.5 0.0 copy-start.7
  195.5 0.0 copy-start.9
  195.5 5.2 %fusion.17 = f32[768,192]{0,1:T(8,128)S(1)} fusion(bf16[768,4096]{1,0:T(8,128)(2,1)} %bitcast.74, bf16[1,192,4096]{2,1,0:T(8,128)(2,1)S(1)} %copy-done.2, f32[768]{0:T(1024)S(1)} %reshape.108), kind=kOutput, calls=%fused_computation.26 | convolution fusion | flops 1208107008 | bytes 8457216 | tf_op jit(solution)/shard_map/dot_general | solution.py:63
  200.7 0.0 copy-done
  200.7 0.0 copy-done.7
  200.7 0.0 copy-done.9
  200.7 3.2 multiply_convert_fusion.6
  203.9 4.4 %convolution_convert_fusion = bf16[768,4096]{1,0:T(8,128)(2,1)} fusion(bf16[768,192]{0,1:T(8,128)(2,1)S(1)} %get-tuple-element.5, bf16[1,192,4096]{2,1,0:T(8,128)(2,1)S(1)} %copy-done.2), kind=kOutput, calls=%fused_computation.2 | convolution fusion | flops 1211105280 | bytes 8159232 | tf_op jit(solution)/shard_map/dot_general | solution.py:89
  208.3 0.0 copy-start.3
  208.3 0.0 reduce-scatter.5.cloned.1.call-update
  208.3 0.2 reduce-scatter.3.cloned.1.call-start
  208.6 1.2 copy-done.3
  209.7 0.0 copy-start.5
  209.7 2.8 fusion.7
  212.6 0.0 copy-done.5
  212.6 5.0 %add_convert_fusion = bf16[768,4096]{1,0:T(8,128)(2,1)} fusion(f32[768,4096]{1,0:T(8,128)S(1)} %fusion.7, bf16[768,192]{0,1:T(8,128)(2,1)S(1)} %copy-done.5, bf16[1,4096,192]{1,2,0:T(8,128)(2,1)S(1)} %copy-done), kind=kOutput, calls=%fused_computation.1 | convolution fusion | flops 1214251008 | bytes 20742144 | tf_op jit(solution)/shard_map/dot_general | solution.py:83
  217.6 0.0 copy-start.1
  217.6 0.0 reduce-scatter.3.cloned.1.call-update
  217.6 60.9 %reduce-scatter.5.cloned.1.call-done = bf16[192,4096]{1,0:T(8,128)(2,1)} async-done(((bf16[768,4096]{1,0:T(8,128)(2,1)}), bf16[192,4096]{1,0:T(8,128)(2,1)}) %reduce-scatter.5.cloned.1.call-update) | async-done | bytes 1572880 | tf_op jit(solution)/shard_map/reduce_scatter | solution.py:90
  278.6 0.0 copy-done.1
  278.6 1.9 fusion.6
  280.5 0.7 convert_element_type.121
  281.1 5.5 %all-to-all-start.4 = ((bf16[8,1,24]{2,1,0:T(2,128)(2,1)}), bf16[8,1,24]{2,1,0:T(2,128)(2,1)S(1)}, u32[]{:S(2)}, u32[]{:S(2)}) async-start(bf16[8,1,24]{2,1,0:T(2,128)(2,1)} %convert_element_type.121), calls=%async_computation.6 | async-start | bytes 8192 | tf_op jit(solution)/shard_map/all_to_all | solution.py:103
  286.6 65.0 %reduce-scatter.3.cloned.1.call-done = bf16[192,4096]{1,0:T(8,128)(2,1)} async-done(((bf16[768,4096]{1,0:T(8,128)(2,1)}), bf16[192,4096]{1,0:T(8,128)(2,1)}) %reduce-scatter.3.cloned.1.call-update) | async-done | bytes 1572880 | tf_op jit(solution)/shard_map/reduce_scatter | solution.py:86
  351.6 0.0 all-to-all-done.4
  351.6 5.5 %all-to-all-start.3 = ((bf16[8,24,4096]{2,1,0:T(8,128)(2,1)}), bf16[8,24,4096]{2,1,0:T(8,128)(2,1)S(1)}, u32[]{:S(2)}, u32[]{:S(2)}) async-start(bf16[8,24,4096]{2,1,0:T(8,128)(2,1)} %bitcast.67), calls=%async_computation.4 | async-start | bytes 3145728 | tf_op jit(solution)/shard_map/all_to_all | solution.py:96
  357.1 5.6 %fusion.3 = bf16[1,4096,192]{1,2,0:T(8,128)(2,1)} fusion(bf16[768,192]{0,1:T(8,128)(2,1)} %get-tuple-element.6, bf16[768,4096]{1,0:T(8,128)(2,1)} %bitcast.71), kind=kOutput, calls=%fused_computation.11 | convolution fusion | flops 1208745984 | bytes 8159232 | tf_op jit(solution)/shard_map/dot_general | solution.py:74
  362.7 0.0 copy-done.6
  362.7 5.5 %fusion.4 = bf16[1,4096,192]{1,2,0:T(8,128)(2,1)} fusion(bf16[768,192]{0,1:T(8,128)(2,1)S(1)} %copy-done.6, bf16[768,4096]{1,0:T(8,128)(2,1)} %bitcast.72), kind=kOutput, calls=%fused_computation.12 | convolution fusion | flops 1208745984 | bytes 8159232 | tf_op jit(solution)/shard_map/dot_general | solution.py:77
  368.2 0.0 slice-done
  368.2 0.0 slice-done.1
  368.2 2.7 fusion.5
  370.9 0.1 reshape.115
  371.0 0.7 fusion.21
  371.7 19.7 %all-to-all-done.3 = bf16[8,24,4096]{2,1,0:T(8,128)(2,1)S(1)} async-done(((bf16[8,24,4096]{2,1,0:T(8,128)(2,1)}), bf16[8,24,4096]{2,1,0:T(8,128)(2,1)S(1)}, u32[]{:S(2)}, u32[]{:S(2)}) %all-to-all-start.3) | async-done | bytes 1572896 | tf_op jit(solution)/shard_map/all_to_all | solution.py:96
  391.4 1.5 convolution_convert_fusion.5
  (7 shorter events, 0.0 us)
Async XLA Ops:
  7.2 193.5 %copy-start = (bf16[1,4096,192]{1,2,0:T(8,128)(2,1)S(1)}, bf16[1,4096,192]{1,2,0:T(8,128)(2,1)}, u32[]{:S(2)}) copy-start(bf16[1,4096,192]{1,2,0:T(8,128)(2,1)} %param.12) | copy-start | bytes 4718596
  7.2 116.3 %all-gather.6.cloned.1.call-start = ((), (), s32[]{:S(2)}) async-start(), calls=%async_computation.8 | async-start | bytes 7864320 | tf_op jit(solution)/shard_map/all_gather | solution.py:45
  9.8 42.2 %copy-start.4 = (bf16[128,4096]{1,0:T(8,128)(2,1)S(1)}, bf16[128,4096]{1,0:T(8,128)(2,1)}, u32[]{:S(2)}) copy-start(bf16[128,4096]{1,0:T(8,128)(2,1)} %param.8) | copy-start | bytes 3145732
  51.9 41.7 %copy-start.8 = (bf16[128,1]{0,1:T(2,128)(2,1)S(1)}, bf16[128,1]{0,1:T(2,128)(2,1)}, u32[]{:S(2)}) copy-start(bf16[128,1]{0,1:T(2,128)(2,1)} %param.10) | copy-start | bytes 772
  51.9 143.6 %all-gather.4.cloned.1.call-start = ((), (), s32[]{:S(2)}) async-start(), calls=%async_computation.7 | async-start | bytes 7864320 | tf_op jit(solution)/shard_map/all_gather | solution.py:46
  93.5 185.0 %reduce-scatter.5.cloned.1.call-start = ((), (), s32[]{:S(2)}) async-start(), calls=%async_computation.10 | async-start | bytes 7864320 | tf_op jit(solution)/shard_map/reduce_scatter | solution.py:90
  123.4 72.0 %copy-start.2 = (bf16[1,192,4096]{2,1,0:T(8,128)(2,1)S(1)}, bf16[1,192,4096]{2,1,0:T(8,128)(2,1)}, u32[]{:S(2)}) copy-start(bf16[1,192,4096]{2,1,0:T(8,128)(2,1)} %param.13) | copy-start | bytes 4718596
  195.5 5.2 %copy-start.7 = (bf16[32,24,4096]{2,1,0:T(8,128)(2,1)S(1)}, bf16[32,24,4096]{2,1,0:T(8,128)(2,1)}, u32[]{:S(2)}) copy-start(bf16[32,24,4096]{2,1,0:T(8,128)(2,1)} %all-gather.6.cloned.1.call-done) | copy-start | bytes 18874372
  195.5 5.2 %copy-start.9 = (f32[768,192]{0,1:T(8,128)S(1)}, f32[768,192]{0,1:T(8,128)}, u32[]{:S(2)}) copy-start(f32[768,192]{0,1:T(8,128)} %fusion.9) | copy-start | bytes 1769476
  208.3 1.4 copy-start.3
  208.3 143.3 %reduce-scatter.3.cloned.1.call-start = ((), (), s32[]{:S(2)}) async-start(), calls=%async_computation.9 | async-start | bytes 7864320 | tf_op jit(solution)/shard_map/reduce_scatter | solution.py:86
  209.7 2.8 copy-start.5
  217.6 61.0 %copy-start.1 = (bf16[8,24,4096]{2,1,0:T(8,128)(2,1)S(1)}, bf16[8,24,4096]{2,1,0:T(8,128)(2,1)}, u32[]{:S(2)}) copy-start(bf16[8,24,4096]{2,1,0:T(8,128)(2,1)} %all_to_all.35) | copy-start | bytes 4718596
  281.1 70.5 %all-to-all-start.4 = ((bf16[8,1,24]{2,1,0:T(2,128)(2,1)}), bf16[8,1,24]{2,1,0:T(2,128)(2,1)S(1)}, u32[]{:S(2)}, u32[]{:S(2)}) async-start(bf16[8,1,24]{2,1,0:T(2,128)(2,1)} %convert_element_type.121), calls=%async_computation.6 | async-start | bytes 8192 | tf_op jit(solution)/shard_map/all_to_all | solution.py:103
  351.6 39.8 %all-to-all-start.3 = ((bf16[8,24,4096]{2,1,0:T(8,128)(2,1)}), bf16[8,24,4096]{2,1,0:T(8,128)(2,1)S(1)}, u32[]{:S(2)}, u32[]{:S(2)}) async-start(bf16[8,24,4096]{2,1,0:T(8,128)(2,1)} %bitcast.67), calls=%async_computation.4 | async-start | bytes 3145728 | tf_op jit(solution)/shard_map/all_to_all | solution.py:96
  357.1 5.6 %copy-start.6 = (bf16[768,192]{0,1:T(8,128)(2,1)S(1)}, bf16[768,192]{0,1:T(8,128)(2,1)}, u32[]{:S(2)}) copy-start(bf16[768,192]{0,1:T(8,128)(2,1)} %get-tuple-element.7) | copy-start | bytes 884740
  357.1 11.1 %slice-start = ((s8[6291456]{0:T(1024)(128)(4,1)}), s8[4194304]{0:T(1024)(128)(4,1)S(1)}, s32[]{:S(2)}) async-start(s8[6291456]{0:T(1024)(128)(4,1)} %bitcast.75), calls=%async_computation.11 | async-start | bytes 8388608
  362.7 5.5 %slice-start.1 = ((s8[6291456]{0:T(1024)(128)(4,1)}), s8[2097152]{0:T(1024)(128)(4,1)S(1)}, s32[]{:S(2)}) async-start(s8[6291456]{0:T(1024)(128)(4,1)} %bitcast.75), calls=%async_computation.12 | async-start | bytes 4194304
Sparse Core Ops, SparseCore 0:
  52.0 71.3 all-gather.5
  125.3 70.1 all-gather.3
  208.5 70.0 reduce-scatter.4
  281.4 70.2 reduce-scatter.2
where the time goes:
time: 404 us; the launch traced here: 399 us
  waiting for transfers between devices  225 us (56%)
  blocking collectives  97.3 us (24%)
  matrix products  45.5 us (11%)
  between operations  13.9 us (3%)
  starting transfers between devices  11.3 us (3%)
  other arithmetic  4.44 us (1%)
    all_gather x1, waiting for transfers between devices, body(): lax.all_gather(recv_dy, 'dp', axis=0, tiled=True)  65.7 us
    reduce_scatter x1, waiting for transfers between devices, body(): lax.psum_scatter(row_part.astype(jnp.bfloat16), 'dp', scatter_dimension=0...  65 us
    reduce_scatter x1, waiting for transfers between devices, body(): lax.psum_scatter(outputs.astype(jnp.bfloat16), 'dp', scatter_dimension=0,...  60.9 us
    all_to_all x1, blocking collectives, body(): lax.all_to_all(sent_dy, 'expert', split_axis=0, concat_axis=0, tiled=True)  41 us
    all_to_all x1, blocking collectives, body(): lax.all_to_all(sent_in, 'expert', split_axis=0, concat_axis=0, tiled=True)  40.2 us
    all_to_all x1, waiting for transfers between devices, body(): lax.all_to_all(own_rows.reshape(expert_count, capacity, width), 'expert',...  19.7 us
    all_gather x1, waiting for transfers between devices, body(): lax.all_gather(recv_in, 'dp', axis=0, tiled=True)  13.4 us
    all_to_all x1, blocking collectives, body(): lax.all_to_all(sent_prob, 'expert', split_axis=0, concat_axis=0, tiled=True)  9.35 us
  transfers between devices with their start and end apart: 6, of which 5 were waited for; matrix products, arithmetic and copies ran while one was open for 8% of the time, Pallas kernels for 0%

commit v1 on v0

v1 whole, which is shorter than its diff:
```python
import functools

import jax
import jax.numpy as jnp
from jax import lax
from jax.experimental import pallas as pl
from jax.experimental.pallas import tpu as pltpu
from jax.sharding import PartitionSpec as P

MESH = pl.DeviceIdType.MESH
LANES = 128
VMEM_LIMIT = 56 * 1024 * 1024


def partner(own, step, count):
    if count & (count - 1):
        return lax.rem(step - own + count, count)
    peer, bit = 0, 1
    while bit < count:
        mine, other = (own // bit) % 2, (step // bit) % 2
        peer = peer + bit * (mine + other - 2 * mine * other)
        bit *= 2
    return peer


def ring_places():
    own = lax.axis_index("dp")
    right = (2 * own + 1) % 5
    return own, right, 3 - right


def greet(count, own_e, right, left):
    barrier = pltpu.get_barrier_semaphore()
    for peer in (right, left):
        pl.semaphore_signal(barrier, inc=1, device_id={"dp": peer}, device_id_type=MESH)

    def step(k, carry):
        pl.semaphore_signal(
            barrier,
            inc=1,
            device_id={"expert": lax.rem(own_e + k, count)},
            device_id_type=MESH,
        )
        return carry

    lax.fori_loop(1, count, step, 0)
    pl.semaphore_wait(barrier, count + 1)


def remote(src, dst, send, recv, axis, peer):
    return pltpu.make_async_remote_copy(
        src_ref=src,
        dst_ref=dst,
        send_sem=send,
        recv_sem=recv,
        device_id={axis: peer},
        device_id_type=MESH,
    )


def spread_kernel(count, sent_in, sent_dy, all_in, all_dy, z_s, z_r, side_s, side_r, far_s, far_r, own_sem):
    own_e = lax.axis_index("expert")
    own_d, right, left = ring_places()
    sent, full = (sent_in, sent_dy), (all_in, all_dy)
    sides = (right, left)

    def z_copy(a, i):
        peer = partner(own_e, i, count)
        return remote(
            sent[a].at[peer], full[a].at[own_d, own_e], z_s.at[a, i], z_r.at[a, i], "expert", peer
        )

    def z_landed(a, i):
        place = full[a].at[own_d, partner(own_e, i, count)]
        return remote(place, place, z_s.at[a, i], z_r.at[a, i], "expert", own_e)

    def side_copy(a, way, i, src=None):
        place = full[a].at[own_d, partner(own_e, i, count)]
        return remote(
            place if src is None else src, place, side_s.at[a, way, i], side_r.at[a, way, i], "dp", sides[way]
        )

    def side_landed(a, way, i):
        place = full[a].at[sides[1 - way], partner(own_e, i, count)]
        return remote(place, place, side_s.at[a, way, i], side_r.at[a, way, i], "dp", sides[way])

    def far_copy(a, i):
        place = full[a].at[sides[1 - a], partner(own_e, i, count)]
        return remote(place, place, far_s.at[a, i], far_r.at[a, i], "dp", sides[a])

    def far_landed(a, i):
        place = full[a].at[3 - own_d, partner(own_e, i, count)]
        return remote(place, place, far_s.at[a, i], far_r.at[a, i], "dp", sides[a])

    own = [
        pltpu.make_async_copy(sent[a].at[own_e], full[a].at[own_d, own_e], own_sem.at[a])
        for a in range(2)
    ]
    for a in range(2):
        own[a].start()
    greet(count, own_e, right, left)
    for a in range(2):
        for way in range(2):
            side_copy(a, way, 0, sent[a].at[own_e]).start()

    def start(i, carry):
        for a in range(2):
            z_copy(a, i).start()
        return carry

    lax.fori_loop(1, count, start, 0)

    def onward(i):
        for a in range(2):
            side_landed(a, a, i).wait_recv()
            far_copy(a, i).start()

    def relay(i, carry):
        for a in range(2):
            z_landed(a, i).wait_recv()
            for way in range(2):
                side_copy(a, way, i).start()
        onward(i - 1)
        return carry

    lax.fori_loop(1, count, relay, 0)
    onward(count - 1)

    def finish(i, carry):
        for a in range(2):
            side_landed(a, 1 - a, i).wait_recv()
            far_landed(a, i).wait_recv()
            far_copy(a, i).wait_send()
            for way in range(2):
                side_copy(a, way, i).wait_send()
        return carry

    lax.fori_loop(0, count, finish, 0)

    def sent_off(i, carry):
        for a in range(2):
            z_copy(a, i).wait_send()
        return carry

    lax.fori_loop(1, count, sent_off, 0)
    for a in range(2):
        own[a].wait()


def spread(sent_in, sent_dy, dp_count):
    count = sent_in.shape[0]
    shape = jax.ShapeDtypeStruct((dp_count,) + sent_in.shape, sent_in.dtype)
    dma = pltpu.SemaphoreType.DMA
    return pl.pallas_call(
        functools.partial(spread_kernel, count),
        out_shape=(shape, shape),
        in_specs=[pl.BlockSpec(memory_space=pl.ANY)] * 2,
        out_specs=[pl.BlockSpec(memory_space=pl.ANY)] * 2,
        scratch_shapes=[
            dma((2, count)),
            dma((2, count)),
            dma((2, 2, count)),
            dma((2, 2, count)),
            dma((2, count)),
            dma((2, count)),
            dma((2,)),
        ],
        compiler_params=pltpu.CompilerParams(
            collective_id=0, has_side_effects=True, vmem_limit_bytes=VMEM_LIMIT
        ),
        name="spread",
    )(sent_in, sent_dy)


def col_tiles(first, last, width):
    while first < last:
        yield slice(first, min(first + width, last))
        first = min(first + width, last)


def gather_kernel(
    count, chunks, gg, gu, score, gate_w, up_w, back, part, far_l, far_r, near_l, near_r, zed,
    far_s, far_rs, side_s, side_rs, sum_s, sum_rs, z_s, z_r, own_sem,
):
    own_e = lax.axis_index("expert")
    own_d, right, left = ring_places()
    width = gate_w.shape[0]
    rows = part.shape[1]
    cols = part.shape[2]
    cap = rows // count
    step_rows = rows // chunks
    slabs = count // chunks
    half = width // 2
    halves = (pl.ds(0, half), pl.ds(half, cols - half))
    spans = ((0, half), (half, cols))
    sides = (right, left)
    far_in = (far_l, far_r)
    near_in = (near_l, near_r)
    targets = (right, left, 3 - own_d, own_d)
    tile = 512

    def rows_at(c):
        return pl.ds(pl.multiple_of(c * step_rows, step_rows), step_rows)

    def far_copy(way, c):
        return remote(
            part.at[2, rows_at(c), halves[way]], far_in[way].at[rows_at(c)],
            far_s.at[way, c], far_rs.at[way, c], "dp", sides[way],
        )

    def side_copy(way, c):
        return remote(
            part.at[way, rows_at(c), halves[1 - way]], near_in[way].at[rows_at(c), halves[1 - way]],
            side_s.at[way, c], side_rs.at[way, c], "dp", sides[way],
        )

    def sum_copy(way, c):
        return remote(
            part.at[way, rows_at(c), halves[way]], near_in[way].at[rows_at(c), halves[way]],
            sum_s.at[way, c], sum_rs.at[way, c], "dp", sides[way],
        )

    def compute(slot):
        row0 = pl.multiple_of(targets[slot] * rows, rows)
        g = gg[pl.ds(row0, rows), :]
        u = gu[pl.ds(row0, rows), :]
        part[slot, :, width:cols] = score[pl.ds(row0, rows), :]

        def one(j, carry):
            at = pl.ds(pl.multiple_of(j * tile, tile), tile)
            dims = (((1,), (1,)), ((), ()))
            value = lax.dot_general(g, gate_w[at, :], dims, preferred_element_type=jnp.float32)
            value = value + lax.dot_general(u, up_w[at, :], dims, preferred_element_type=jnp.float32)
            part[slot, :, at] = value.astype(part.dtype)
            return carry

        lax.fori_loop(0, width // tile, one, 0)

    def for_chunks(f):
        def go(c, carry):
            f(c)
            return carry

        lax.fori_loop(0, chunks, go, 0)

    greet(count, own_e, right, left)
    compute(2)

    @for_chunks
    def _(c):
        for way in range(2):
            far_copy(way, c).start()

    for way in range(2):
        compute(way)

        @for_chunks
        def _(c):
            side_copy(way, c).start()

    compute(3)

    @for_chunks
    def _(c):
        for way in range(2):
            far_copy(way, c).wait_recv()
            for at in col_tiles(*spans[way], tile):
                there = slice(at.start - spans[way][0], at.stop - spans[way][0])
                total = part[way, rows_at(c), at].astype(jnp.float32) + far_in[way][
                    rows_at(c), there
                ].astype(jnp.float32)
                part[way, rows_at(c), at] = total.astype(part.dtype)
            sum_copy(way, c).start()

    def z_copy(i):
        peer = partner(own_e, i, count)
        return remote(zed.at[peer], back.at[own_e], z_s.at[i], z_r.at[i], "expert", peer)

    def z_landed(i):
        place = back.at[partner(own_e, i, count)]
        return remote(place, place, z_s.at[i], z_r.at[i], "expert", own_e)

    def merge(c):
        for way in range(2):
            side_copy(way, c).wait_recv()
            sum_copy(way, c).wait_recv()
        for at in col_tiles(0, cols, tile):
            total = part[3, rows_at(c), at].astype(jnp.float32)
            total = total + near_l[rows_at(c), at].astype(jnp.float32)
            total = total + near_r[rows_at(c), at].astype(jnp.float32)
            total = total.reshape(slabs, cap, at.stop - at.start)
            zed[pl.ds(c * slabs, slabs), :, at] = total.astype(zed.dtype)

    @for_chunks
    def _(c):
        merge(c)
        for k in range(slabs):
            there = c * slabs + k
            step = partner(own_e, there, count)

            @pl.when(there != own_e)
            def _():
                z_copy(step).start()

    own = pltpu.make_async_copy(zed.at[own_e], back.at[own_e], own_sem.at[0])
    own.start()
    own.wait()

    def landed(i, carry):
        z_landed(i).wait_recv()
        z_copy(i).wait_send()
        return carry

    lax.fori_loop(1, count, landed, 0)

    @for_chunks
    def _(c):
        for way in range(2):
            far_copy(way, c).wait_send()
            side_copy(way, c).wait_send()
            sum_copy(way, c).wait_send()


def gather(gg, gu, score, gate_w, up_w, count, dp_count):
    width = gate_w.shape[0]
    rows = gg.shape[0] // dp_count
    cols = width + LANES
    half = width // 2
    chunks = 4 if count % 4 == 0 and (rows // 4) % 16 == 0 else 1
    dma = pltpu.SemaphoreType.DMA
    kind = jnp.bfloat16
    pairs = dma((2, chunks))
    return pl.pallas_call(
        functools.partial(gather_kernel, count, chunks),
        out_shape=jax.ShapeDtypeStruct((count, rows // count, cols), kind),
        in_specs=[pl.BlockSpec(memory_space=pltpu.VMEM)] * 5,
        out_specs=pl.BlockSpec(memory_space=pl.ANY),
        scratch_shapes=[
            pltpu.VMEM((4, rows, cols), kind),
            pltpu.VMEM((rows, half), kind),
            pltpu.VMEM((rows, cols - half), kind),
            pltpu.VMEM((rows, cols), kind),
            pltpu.VMEM((rows, cols), kind),
            pltpu.VMEM((count, rows // count, cols), kind),
            pairs,
            pairs,
            pairs,
            pairs,
            pairs,
            pairs,
            dma((count,)),
            dma((count,)),
            dma((1,)),
        ],
        compiler_params=pltpu.CompilerParams(
            collective_id=1, has_side_effects=True, vmem_limit_bytes=VMEM_LIMIT
        ),
        name="gather",
    )(gg, gu, score, gate_w, up_w)


def body(tokens, out_grad, routes, gate_probs, w_gate, w_up, w_down):
    expert_count = lax.axis_size("expert")
    dp_count = lax.axis_size("dp")
    tok_count, width = tokens.shape
    top_count = routes.shape[1]
    capacity = 3 * tok_count * top_count // (2 * expert_count)
    capacity = -(-capacity // 8) * 8
    slot_total = expert_count * capacity
    flat_routes = routes.reshape(-1)
    order = jnp.arange(flat_routes.shape[0], dtype=jnp.int32)
    same = (flat_routes[:, None] == flat_routes[None, :]) & (order[None, :] < order[:, None])
    slot_index = jnp.sum(same.astype(jnp.int32), axis=1)
    destination = flat_routes * capacity + slot_index
    placing = jnp.arange(slot_total, dtype=jnp.int32)[:, None] == destination[None, :]
    weights = gate_probs.reshape(-1).astype(jnp.float32)
    by_token = placing.astype(jnp.bfloat16).reshape(slot_total, tok_count, top_count)
    collect = jnp.sum(by_token, axis=2)
    weighted = jnp.where(placing, weights[None, :], 0.0).astype(jnp.bfloat16)
    collect_weighted = jnp.sum(weighted.reshape(slot_total, tok_count, top_count), axis=2)
    sent_shape = (expert_count, capacity, width)
    sent_in = (
        jnp.dot(collect, tokens, preferred_element_type=jnp.float32)
        .astype(jnp.bfloat16)
        .reshape(sent_shape)
    )
    sent_dy = (
        jnp.dot(collect_weighted, out_grad, preferred_element_type=jnp.float32)
        .astype(jnp.bfloat16)
        .reshape(sent_shape)
    )
    all_in, all_dy = spread(sent_in, sent_dy, dp_count)
    row_total = dp_count * slot_total
    rows_in = all_in.reshape(row_total, width)
    scaled = all_dy.reshape(row_total, width)
    gate_w = w_gate[0]
    up_w = w_up[0]
    down_w = w_down[0]
    contract_last = (((1,), (1,)), ((), ()))
    contract_first = (((0,), (0,)), ((), ()))
    gate_pre = jnp.dot(rows_in, gate_w, preferred_element_type=jnp.float32)
    up_pre = jnp.dot(rows_in, up_w, preferred_element_type=jnp.float32)
    sigmoid_gate = jax.nn.sigmoid(gate_pre)
    active = gate_pre * sigmoid_gate
    hidden = (active * up_pre).astype(jnp.bfloat16)
    back_hidden = lax.dot_general(scaled, down_w, contract_last, preferred_element_type=jnp.float32)
    grad_gate_pre = (
        back_hidden * up_pre * sigmoid_gate * (1.0 + gate_pre * (1.0 - sigmoid_gate))
    ).astype(jnp.bfloat16)
    grad_up_pre = (back_hidden * active).astype(jnp.bfloat16)
    score = jnp.sum(back_hidden * hidden.astype(jnp.float32), axis=1, keepdims=True)
    score = jnp.broadcast_to(score, (row_total, LANES)).astype(jnp.bfloat16)
    back = gather(grad_gate_pre, grad_up_pre, score, gate_w, up_w, expert_count, dp_count)
    grad_down = lax.dot_general(
        hidden, scaled, contract_first, preferred_element_type=jnp.float32
    ).astype(jnp.bfloat16)
    grad_gate = lax.dot_general(
        rows_in, grad_gate_pre, contract_first, preferred_element_type=jnp.float32
    ).astype(jnp.bfloat16)
    grad_up = lax.dot_general(
        rows_in, grad_up_pre, contract_first, preferred_element_type=jnp.float32
    ).astype(jnp.bfloat16)
    back = back.reshape(slot_total, width + LANES)
    grad_tokens = lax.dot_general(
        collect, back[:, :width], contract_first, preferred_element_type=jnp.float32
    ).astype(jnp.bfloat16)
    picked = lax.dot_general(
        placing.astype(jnp.bfloat16),
        back[:, width:],
        contract_first,
        preferred_element_type=jnp.float32,
    )[:, 0]
    grad_probs = (picked / weights).astype(jnp.bfloat16).reshape(tok_count, top_count)
    return (grad_tokens, grad_probs, grad_gate[None], grad_up[None], grad_down[None])


def solution(mesh):
    in_specs = (
        P(("dp", "expert"), None),
        P(("dp", "expert"), None),
        P(("dp", "expert"), None),
        P(("dp", "expert"), None),
        P("expert", None, "dp"),
        P("expert", None, "dp"),
        P("expert", "dp", None),
    )
    out_specs = (
        P(("dp", "expert"), None),
        P(("dp", "expert"), None),
        P("expert", None, "dp"),
        P("expert", None, "dp"),
        P("expert", "dp", None),
    )
    return jax.shard_map(body, mesh=mesh, in_specs=in_specs, out_specs=out_specs, check_vma=False)
```

time: 404 us -> 257 us (0.64)
  waiting for transfers between devices: 225 us -> 0 us
  Pallas kernels: 0 us -> 200 us
  blocking collectives: 97.3 us -> 0 us
  between operations: 13.9 us -> 0.77 us
  local copies, waits for them, and re-layouts: 2.16 us -> 13.8 us
  starting transfers between devices: 11.3 us -> 0 us
  matrix products: 45.5 us -> 37.2 us
    pallas_call x0 -> x2, Pallas kernels: none -> 200 us  [the longest x1 108 us: spread(): pl.pallas_call(functools.partial(spread_kernel, count), out_shape=(shape,...]
    reduce_scatter x2 -> x0, waiting for transfers between devices: 126 us -> none  [the longest x1 65 us: body(): lax.psum_scatter(row_part.astype(jnp.bfloat16), 'dp', scatter_dimension=0...]
    all_to_all x3 -> x0, blocking collectives: 90.6 us -> none  [the longest x1 41 us: body(): lax.all_to_all(sent_dy, 'expert', split_axis=0, concat_axis=0, tiled=True)]
    all_gather x2 -> x0, waiting for transfers between devices: 79.1 us -> none  [the longest x1 65.7 us: body(): lax.all_gather(recv_dy, 'dp', axis=0, tiled=True)]
    all_to_all x2 -> x0, waiting for transfers between devices: 19.7 us -> none  [the longest x1 19.7 us: body(): lax.all_to_all(own_rows.reshape(expert_count, capacity, width), 'expert',...]
    all_to_all x2 -> x0, starting transfers between devices: 11 us -> none  [the longest x1 5.48 us: body(): lax.all_to_all(own_rows.reshape(expert_count, capacity, width), 'expert',...]
    dot_general x8 -> x4, matrix products: 20.3 us -> 9.31 us  [the longest x1 3.24 us: body(): lax.dot_general(scaled, down_w, contract_last, preferred_element_type=jnp...]
    all_gather x1 -> x0, blocking collectives: 6.73 us -> none  [body(): lax.all_gather(recv_prob, 'dp', axis=0, tiled=True)]
  transfers between devices with their start and end apart: 6 -> 0, of which waited for: 5 -> 0; matrix products, arithmetic and copies ran while one was open for 8% -> 0% of each run, Pallas kernels for 0% -> 0%
where the time goes in v1:
time: 257 us; the launch traced here: 254 us
  Pallas kernels  200 us (78%)
  matrix products  37.2 us (14%)
  local copies, waits for them, and re-layouts  13.8 us (5%)
    pallas_call x1, Pallas kernels, spread(): pl.pallas_call(functools.partial(spread_kernel, count), out_shape=(shape,...  108 us
    pallas_call x1, Pallas kernels, gather(): pl.pallas_call(functools.partial(gather_kernel, count, chunks), out_shape...  92.7 us
    unnamed x22, local copies, waits for them, and re-layouts  6.3 us
    dot_general x1, matrix products, body(): gate_pre = jnp.dot(rows_in, gate_w, preferred_element_type=jnp.float32)  6.15 us
    dot_general x1, matrix products, body(): lax.dot_general(hidden, scaled, contract_first, preferred_element_type=jn...  5.68 us
    dot_general x1, matrix products, body(): lax.dot_general(rows_in, grad_up_pre, contract_first, preferred_element_t...  5.37 us
    dot_general x1, matrix products, body(): up_pre = jnp.dot(rows_in, up_w, preferred_element_type=jnp.float32)  5.15 us

profile of v1, /device:TPU:11, one launch (start us, length us, event | category | flops | bytes accessed | tf_op | source)
XLA Modules:
  0.0 253.8 jit_solution(16199481305570808946)
XLA Ops:
  0.6 0.0 copy-start
  0.6 0.0 copy-start.7
  0.7 0.0 copy-start.3
  0.7 1.0 convert_reduce_fusion
  1.7 0.7 multiply_add_fusion
  2.3 2.9 %convolution_convert_fusion.4 = bf16[192,4096]{1,0:T(8,128)(2,1)} fusion(bf16[128,4096]{1,0:T(8,128)(2,1)} %param.7, s32[128]{0:T(128)S(1)} %multiply_add_fusion), kind=kOutput, calls=%fused_computation.4 | convolution fusion | flops 202137600 | bytes 2621952 | tf_op jit(solution)/shard_map/dot_general | solution.py:383
  5.3 0.0 copy-done.7
  5.3 0.0 copy-done.3
  5.3 1.7 convolution_convert_fusion.3
  7.0 0.0 copy-start.2
  7.0 107.6 %spread.1 = (bf16[4,8,24,4096]{3,2,1,0:T(8,128)(2,1)}, bf16[4,8,24,4096]{3,2,1,0:T(8,128)(2,1)}) custom-call(bf16[8,24,4096]{2,1,0:T(8,128)(2,1)} %bitcast.48, bf16[8,24,4096]{2,1,0:T(8,128)(2,1)} %bitcast.49), custom_call_target="tpu_custom_call" | custom-call | tf_op jit(solution)/shard_map/spread/pallas_call | solution.py:154
  114.6 0.0 copy-done.2
  114.6 0.0 copy-start.1
  114.6 5.1 %fusion.6 = f32[768,192]{0,1:T(8,128)S(1)} fusion(bf16[768,4096]{1,0:T(8,128)(2,1)} %bitcast.51, bf16[1,4096,192]{1,2,0:T(8,128)(2,1)S(1)} %copy-done.2), kind=kOutput, calls=%fused_computation.12 | convolution fusion | flops 1207959552 | bytes 8454144 | tf_op jit(solution)/shard_map/dot_general | solution.py:402
  119.7 0.0 copy-start.4
  119.7 0.0 copy-done
  119.8 0.0 copy-done.1
  119.8 3.2 %fusion.21 = (f32[768,192]{0,1:T(8,128)}, f32[768,192]{0,1:T(8,128)}) fusion(f32[768,192]{0,1:T(8,128)S(1)} %fusion.6, bf16[768,4096]{1,0:T(8,128)(2,1)S(1)} %bitcast.43, bf16[1,192,4096]{2,1,0:T(8,128)(2,1)S(1)} %copy-done), kind=kOutput, calls=%fused_computation.39 | convolution fusion | flops 1208107008 | bytes 9633792 | tf_op jit(solution)/shard_map/dot_general | solution.py:406
  123.0 0.0 copy-done.4
  123.0 2.2 copy.35
  125.2 2.2 copy.38
  127.4 2.2 copy.39
  129.6 0.0 slice-start
  129.6 6.1 %multiply_reduce_fusion = (bf16[768]{0:T(1024)(128)(2,1)S(1)}, bf16[768,192]{1,0:T(8,128)(2,1)S(1)}, bf16[768,192]{1,0:T(8,128)(2,1)S(1)}, bf16[768,192]{1,0:T(8,128)(2,1)S(1)}) fusion(f32[768,192]{1,0:T(8,128)} %copy.38, f32[768,192]{1,0:T(8,128)} %copy.39, f32[768,192]{1,0:T(8,128)} %copy.35, bf16[768,4096]{1,0:T(8,128)(2,1)} %bitcast.52, ...), kind=kOutput, calls=%fused_computation.18 | convolution fusion | flops 1210465536 | bytes 10520064 | tf_op jit(solution)/shard_map/dot_general | solution.py:401
  135.8 0.0 copy-start.5
  135.8 0.0 copy-start.6
  135.8 0.0 slice-start.1
  135.8 5.7 %fusion.2 = bf16[1,192,4096]{2,1,0:T(8,128)(2,1)} fusion(bf16[768,192]{1,0:T(8,128)(2,1)S(1)} %get-tuple-element.10, bf16[768,4096]{1,0:T(8,128)(2,1)} %bitcast.42), kind=kOutput, calls=%fused_computation.8 | convolution fusion | flops 1208745984 | bytes 8159232 | tf_op jit(solution)/shard_map/dot_general | solution.py:414
  141.5 0.0 copy-done.5
  141.5 5.4 %fusion.1 = bf16[1,4096,192]{1,2,0:T(8,128)(2,1)} fusion(bf16[768,4096]{1,0:T(8,128)(2,1)} %bitcast.53, bf16[768,192]{1,0:T(8,128)(2,1)S(1)} %get-tuple-element.11.gu), kind=kOutput, calls=%fused_computation.7 | convolution fusion | flops 1208745984 | bytes 8159232 | tf_op jit(solution)/shard_map/dot_general | solution.py:420
  146.9 0.0 copy-done.6
  146.9 0.0 slice-done
  146.9 0.0 slice-done.1
  146.9 2.7 %fusion = bf16[1,4096,192]{1,2,0:T(8,128)(2,1)} fusion(bf16[768,4096]{1,0:T(8,128)(2,1)S(1)} %bitcast.56, bf16[768,192]{1,0:T(8,128)(2,1)S(1)} %get-tuple-element.12.gg), kind=kOutput, calls=%fused_computation.6 | convolution fusion | flops 1208745984 | bytes 8159232 | tf_op jit(solution)/shard_map/dot_general | solution.py:417
  149.6 0.8 broadcast_in_dim.34.score
  150.4 2.4 copy.32
  152.8 3.8 %copy.33 = bf16[1,4096,192]{2,1,0:T(8,128)(2,1)} copy(bf16[1,4096,192]{1,2,0:T(8,128)(2,1)} %param.11) | data formatting | bytes 3145728 | tf_op args[4]
  156.6 92.7 %gather.1 = bf16[8,24,4224]{2,1,0:T(8,128)(2,1)} custom-call(bf16[768,192]{1,0:T(8,128)(2,1)} %copy-done.6, bf16[768,192]{1,0:T(8,128)(2,1)} %copy-done.5, bf16[768,128]{1,0:T(8,128)(2,1)} %broadcast_in_dim.34.score, bf16[4096,192]{1,0:T(8,128)(2,1)} %bitcast.45, bf16[4096,192]{1,0:T(8,128)(2,1)} %bitcast.44), custom_call_target="tpu_custom_call" | custom-call | tf_op jit(solution)/shard_map/gather/pallas_call | solution.py:333
  249.4 2.9 %convolution_convert_fusion.5 = bf16[128,4096]{1,0:T(8,128)(2,1)} fusion(bf16[192,4224]{1,0:T(8,128)(2,1)} %bitcast.46, s32[128]{0:T(128)S(1)} %multiply_add_fusion), kind=kOutput, calls=%fused_computation.5 | convolution fusion | flops 201875456 | bytes 2621952 | tf_op jit(solution)/shard_map/dot_general | solution.py:424
  252.3 1.5 fusion.10
  (1 shorter events, 0.0 us)
Async XLA Ops:
  0.6 119.1 %copy-start = (bf16[1,192,4096]{2,1,0:T(8,128)(2,1)S(1)}, bf16[1,192,4096]{2,1,0:T(8,128)(2,1)}, u32[]{:S(2)}) copy-start(bf16[1,192,4096]{2,1,0:T(8,128)(2,1)} %param.13) | copy-start | bytes 4718596
  0.6 4.6 %copy-start.7 = (bf16[128,1]{0,1:T(2,128)(2,1)S(1)}, bf16[128,1]{0,1:T(2,128)(2,1)}, u32[]{:S(2)}) copy-start(bf16[128,1]{0,1:T(2,128)(2,1)} %param.10) | copy-start | bytes 772
  0.7 4.6 %copy-start.3 = (bf16[128,4096]{1,0:T(8,128)(2,1)S(1)}, bf16[128,4096]{1,0:T(8,128)(2,1)}, u32[]{:S(2)}) copy-start(bf16[128,4096]{1,0:T(8,128)(2,1)} %param.8) | copy-start | bytes 3145732
  7.0 107.6 %copy-start.2 = (bf16[1,4096,192]{1,2,0:T(8,128)(2,1)S(1)}, bf16[1,4096,192]{1,2,0:T(8,128)(2,1)}, u32[]{:S(2)}) copy-start(bf16[1,4096,192]{1,2,0:T(8,128)(2,1)} %param.12) | copy-start | bytes 4718596
  114.6 5.2 %copy-start.1 = (bf16[4,8,24,4096]{3,2,1,0:T(8,128)(2,1)S(1)}, bf16[4,8,24,4096]{3,2,1,0:T(8,128)(2,1)}, u32[]{:S(2)}) copy-start(bf16[4,8,24,4096]{3,2,1,0:T(8,128)(2,1)} %get-tuple-element.7) | copy-start | bytes 18874372
  119.7 3.3 %copy-start.4 = (f32[768,192]{0,1:T(8,128)}, f32[768,192]{0,1:T(8,128)S(1)}, u32[]{:S(2)}) copy-start(f32[768,192]{0,1:T(8,128)S(1)} %fusion.6) | copy-start | bytes 1769476
  129.6 17.2 %slice-start = ((s8[6291456]{0:T(1024)(128)(4,1)}), s8[4194304]{0:T(1024)(128)(4,1)S(1)}, s32[]{:S(2)}) async-start(s8[6291456]{0:T(1024)(128)(4,1)} %bitcast.54), calls=%async_computation | async-start | bytes 8388608
  135.8 5.7 %copy-start.5 = (bf16[768,192]{1,0:T(8,128)(2,1)}, bf16[768,192]{1,0:T(8,128)(2,1)S(1)}, u32[]{:S(2)}) copy-start(bf16[768,192]{1,0:T(8,128)(2,1)S(1)} %get-tuple-element.11.gu) | copy-start | bytes 884740
  135.8 11.1 %copy-start.6 = (bf16[768,192]{1,0:T(8,128)(2,1)}, bf16[768,192]{1,0:T(8,128)(2,1)S(1)}, u32[]{:S(2)}) copy-start(bf16[768,192]{1,0:T(8,128)(2,1)S(1)} %get-tuple-element.12.gg) | copy-start | bytes 884740
  135.8 11.1 %slice-start.1 = ((s8[6291456]{0:T(1024)(128)(4,1)}), s8[2097152]{0:T(1024)(128)(4,1)S(1)}, s32[]{:S(2)}) async-start(s8[6291456]{0:T(1024)(128)(4,1)} %bitcast.54), calls=%async_computation.1 | async-start | bytes 4194304

commit v2 on v1

--- a/solution.py
+++ b/solution.py
@@ -9,7 +9,7 @@
 
 MESH = pl.DeviceIdType.MESH
 LANES = 128
-VMEM_LIMIT = 56 * 1024 * 1024
+VMEM_LIMIT = 60 * 1024 * 1024
 
 
 def partner(own, step, count):
@@ -359,6 +359,298 @@
     )(gg, gu, score, gate_w, up_w)
 
 
+def fused_kernel(
+    count, sent_in, sent_dy, gate_w, up_w, down_w,
+    all_in, all_dy, back, grad_gate, grad_up, grad_down,
+    stage, flat_in, flat_dy, hid, dgate, dup, part, far_l, far_r, near_l, near_r, zed,
+    z_s, z_r, side_s, side_r, far_s, far_r_sem, own_sem, stage_sem,
+    rf_s, rf_r, rd_s, rd_r, rs_s, rs_r, home_s, home_r,
+):
+    own_e = lax.axis_index("expert")
+    own_d, right, left = ring_places()
+    sent, full, flat = (sent_in, sent_dy), (all_in, all_dy), (flat_in, flat_dy)
+    sides = (right, left)
+    dp_count, _, cap, width = all_in.shape
+    cols = part.shape[3]
+    group = dp_count * cap
+    half = width // 2
+    halves = (pl.ds(0, half), pl.ds(half, cols - half))
+    spans = ((0, half), (half, cols))
+    far_in, near_in = (far_l, far_r), (near_l, near_r)
+    tile = 512
+    last_dims = (((1,), (1,)), ((), ()))
+    first_dims = (((0,), (0,)), ((), ()))
+
+    def z_copy(a, i):
+        peer = partner(own_e, i, count)
+        return remote(
+            sent[a].at[peer], full[a].at[own_d, own_e], z_s.at[a, i], z_r.at[a, i], "expert", peer
+        )
+
+    def z_landed(a, i):
+        place = full[a].at[own_d, partner(own_e, i, count)]
+        return remote(place, place, z_s.at[a, i], z_r.at[a, i], "expert", own_e)
+
+    def side_copy(a, way, i, src=None):
+        place = full[a].at[own_d, partner(own_e, i, count)]
+        return remote(
+            place if src is None else src, place, side_s.at[a, way, i], side_r.at[a, way, i], "dp", sides[way]
+        )
+
+    def side_landed(a, way, i):
+        place = full[a].at[sides[1 - way], partner(own_e, i, count)]
+        return remote(place, place, side_s.at[a, way, i], side_r.at[a, way, i], "dp", sides[way])
+
+    def onward_copy(a, i):
+        place = full[a].at[sides[1 - a], partner(own_e, i, count)]
+        return remote(place, place, far_s.at[a, i], far_r_sem.at[a, i], "dp", sides[a])
+
+    def onward_landed(a, i):
+        place = full[a].at[3 - own_d, partner(own_e, i, count)]
+        return remote(place, place, far_s.at[a, i], far_r_sem.at[a, i], "dp", sides[a])
+
+    def rf_copy(way, c):
+        return remote(
+            part.at[3 - own_d, c, :, halves[way]], far_in[way].at[c],
+            rf_s.at[way, c], rf_r.at[way, c], "dp", sides[way],
+        )
+
+    def rd_copy(way, c):
+        return remote(
+            part.at[sides[way], c, :, halves[1 - way]], near_in[way].at[c, :, halves[1 - way]],
+            rd_s.at[way, c], rd_r.at[way, c], "dp", sides[way],
+        )
+
+    def rs_copy(way, c):
+        return remote(
+            part.at[sides[way], c, :, halves[way]], near_in[way].at[c, :, halves[way]],
+            rs_s.at[way, c], rs_r.at[way, c], "dp", sides[way],
+        )
+
+    def home_copy(i):
+        peer = partner(own_e, i, count)
+        return remote(zed.at[i], back.at[own_e], home_s.at[i], home_r.at[i], "expert", peer)
+
+    def home_landed(i):
+        place = back.at[partner(own_e, i, count)]
+        return remote(place, place, home_s.at[i], home_r.at[i], "expert", own_e)
+
+    own = [
+        pltpu.make_async_copy(sent[a].at[own_e], full[a].at[own_d, own_e], own_sem.at[a])
+        for a in range(2)
+    ]
+    for a in range(2):
+        own[a].start()
+    greet(count, own_e, right, left)
+    for a in range(2):
+        for way in range(2):
+            side_copy(a, way, 0, sent[a].at[own_e]).start()
+
+    def start(i, carry):
+        for a in range(2):
+            z_copy(a, i).start()
+        return carry
+
+    lax.fori_loop(1, count, start, 0)
+    for a in range(2):
+        own[a].wait()
+
+    def relay(i):
+        for a in range(2):
+            z_landed(a, i).wait_recv()
+            for way in range(2):
+                side_copy(a, way, i).start()
+
+    def onward(i):
+        for a in range(2):
+            side_landed(a, a, i).wait_recv()
+            onward_copy(a, i).start()
+
+    def compute(i):
+        src = partner(own_e, i, count)
+        for a in range(2):
+            side_landed(a, 1 - a, i).wait_recv()
+            onward_landed(a, i).wait_recv()
+        loads = [
+            pltpu.make_async_copy(full[a].at[:, src], stage.at[a], stage_sem.at[a])
+            for a in range(2)
+        ]
+        for load in loads:
+            load.start()
+        for load in loads:
+            load.wait()
+        rows = pl.ds(pl.multiple_of(i * group, group), group)
+        for a in range(2):
+            for at in col_tiles(0, width, tile):
+                value = stage[a, :, :, at].astype(jnp.float32).reshape(group, tile)
+                flat[a][rows, at] = value.astype(flat[a].dtype)
+
+        def product(x, w):
+            return lax.dot_general(x, w, last_dims, preferred_element_type=jnp.float32)
+
+        gate_pre = product(flat_in[rows, :], gate_w[...])
+        up_pre = product(flat_in[rows, :], up_w[...])
+        back_hidden = product(flat_dy[rows, :], down_w[...])
+        sigmoid_gate = jax.nn.sigmoid(gate_pre)
+        active = gate_pre * sigmoid_gate
+        hidden = (active * up_pre).astype(jnp.bfloat16)
+        score = jnp.sum(back_hidden * hidden.astype(jnp.float32), axis=1, keepdims=True)
+        g = (back_hidden * up_pre * sigmoid_gate * (1.0 + gate_pre * (1.0 - sigmoid_gate))).astype(
+            jnp.bfloat16
+        )
+        u = (back_hidden * active).astype(jnp.bfloat16)
+        hid[rows, :] = hidden
+        dgate[rows, :] = g
+        dup[rows, :] = u
+        score = jnp.broadcast_to(score, (group, cols - width)).reshape(dp_count, cap, cols - width)
+        part[:, i, :, width:cols] = score.astype(part.dtype)
+        for at in col_tiles(0, width, tile):
+            value = jnp.dot(g, gate_w[:, at], preferred_element_type=jnp.float32)
+            value = value + jnp.dot(u, up_w[:, at], preferred_element_type=jnp.float32)
+            part[:, i, :, at] = value.reshape(dp_count, cap, tile).astype(part.dtype)
+        for way in range(2):
+            rf_copy(way, i).start()
+        for way in range(2):
+            rd_copy(way, i).start()
+
+    def ring_sum(i):
+        for way in range(2):
+            rf_copy(way, i).wait_recv()
+            for at in col_tiles(*spans[way], tile):
+                there = slice(at.start - spans[way][0], at.stop - spans[way][0])
+                total = part[sides[way], i, :, at].astype(jnp.float32)
+                total = total + far_in[way][i, :, there].astype(jnp.float32)
+                part[sides[way], i, :, at] = total.astype(part.dtype)
+            rs_copy(way, i).start()
+
+    def merge(i):
+        for way in range(2):
+            rd_copy(way, i).wait_recv()
+            rs_copy(way, i).wait_recv()
+        for at in col_tiles(0, cols, tile):
+            total = part[own_d, i, :, at].astype(jnp.float32)
+            total = total + near_l[i, :, at].astype(jnp.float32)
+            total = total + near_r[i, :, at].astype(jnp.float32)
+            zed[i, :, at] = total.astype(zed.dtype)
+
+        @pl.when(i > 0)
+        def _():
+            home_copy(i).start()
+
+    def weight_grad(out, left_rows, right_rows):
+        def one(j, carry):
+            at = pl.ds(pl.multiple_of(j * tile, tile), tile)
+            value = lax.dot_general(
+                left_rows[...], right_rows[:, at], first_dims, preferred_element_type=jnp.float32
+            )
+            out[:, at] = value.astype(out.dtype)
+            return carry
+
+        lax.fori_loop(0, width // tile, one, 0)
+
+    grads = ((grad_down, hid, flat_dy), (grad_gate, dgate, flat_in), (grad_up, dup, flat_in))
+
+    def step(t, carry):
+        def during(lag, first, f):
+            @pl.when((t - lag >= first) & (t - lag < count))
+            def _():
+                f(t - lag)
+
+        during(0, 1, relay)
+        during(1, 0, onward)
+        during(3, 0, ring_sum)
+        during(2, 0, compute)
+        during(4, 0, merge)
+        for k, grad in enumerate(grads):
+            @pl.when(t == count + 2 + (k + 1) // 2)
+            def _():
+                weight_grad(*grad)
+
+        return carry
+
+    lax.fori_loop(0, count + 4, step, 0)
+    keep = pltpu.make_async_copy(zed.at[0], back.at[own_e], own_sem.at[0])
+    keep.start()
+    keep.wait()
+
+    def finish(i, carry):
+        for a in range(2):
+            onward_copy(a, i).wait_send()
+            for way in range(2):
+                side_copy(a, way, i).wait_send()
+        for way in range(2):
+            rf_copy(way, i).wait_send()
+            rd_copy(way, i).wait_send()
+            rs_copy(way, i).wait_send()
+        return carry
+
+    lax.fori_loop(0, count, finish, 0)
+
+    def landed(i, carry):
+        for a in range(2):
+            z_copy(a, i).wait_send()
+        home_landed(i).wait_recv()
+        home_copy(i).wait_send()
+        return carry
+
+    lax.fori_loop(1, count, landed, 0)
+
+
+def fused(sent_in, sent_dy, gate_t, up_t, down_w, dp_count):
+    count, cap, width = sent_in.shape
+    kind = sent_in.dtype
+    hidden = down_w.shape[0]
+    cols, half = width + LANES, width // 2
+    total = dp_count * count * cap
+    dma = pltpu.SemaphoreType.DMA
+    full = jax.ShapeDtypeStruct((dp_count, count, cap, width), kind)
+    grad = jax.ShapeDtypeStruct((hidden, width), kind)
+    whole = pl.BlockSpec(memory_space=pltpu.VMEM)
+    apart = pl.BlockSpec(memory_space=pl.ANY)
+    pair = dma((2, count))
+    results = pl.pallas_call(
+        functools.partial(fused_kernel, count),
+        out_shape=(full, full, jax.ShapeDtypeStruct((count, cap, cols), kind), grad, grad, grad),
+        in_specs=[apart, apart, whole, whole, whole],
+        out_specs=[apart, apart, apart, whole, whole, whole],
+        scratch_shapes=[
+            pltpu.VMEM((2, dp_count, cap, width), kind),
+            pltpu.VMEM((total, width), kind),
+            pltpu.VMEM((total, width), kind),
+            pltpu.VMEM((total, hidden), kind),
+            pltpu.VMEM((total, hidden), kind),
+            pltpu.VMEM((total, hidden), kind),
+            pltpu.VMEM((dp_count, count, cap, cols), kind),
+            pltpu.VMEM((count, cap, half), kind),
+            pltpu.VMEM((count, cap, cols - half), kind),
+            pltpu.VMEM((count, cap, cols), kind),
+            pltpu.VMEM((count, cap, cols), kind),
+            pltpu.VMEM((count, cap, cols), kind),
+            pair,
+            pair,
+            dma((2, 2, count)),
+            dma((2, 2, count)),
+            pair,
+            pair,
+            dma((2,)),
+            dma((2,)),
+            pair,
+            pair,
+            pair,
+            pair,
+            pair,
+            pair,
+            dma((count,)),
+            dma((count,)),
+        ],
+        compiler_params=pltpu.CompilerParams(
+            collective_id=2, has_side_effects=True, vmem_limit_bytes=VMEM_LIMIT
+        ),
+        name="fused",
+    )(sent_in, sent_dy, gate_t, up_t, down_w)
+    return results[2:]
+
+
 def body(tokens, out_grad, routes, gate_probs, w_gate, w_up, w_down):
     expert_count = lax.axis_size("expert")
     dp_count = lax.axis_size("dp")
@@ -389,37 +681,43 @@
         .astype(jnp.bfloat16)
         .reshape(sent_shape)
     )
-    all_in, all_dy = spread(sent_in, sent_dy, dp_count)
+    contract_first = (((0,), (0,)), ((), ()))
     row_total = dp_count * slot_total
-    rows_in = all_in.reshape(row_total, width)
-    scaled = all_dy.reshape(row_total, width)
-    gate_w = w_gate[0]
-    up_w = w_up[0]
-    down_w = w_down[0]
-    contract_last = (((1,), (1,)), ((), ()))
-    contract_first = (((0,), (0,)), ((), ()))
-    gate_pre = jnp.dot(rows_in, gate_w, preferred_element_type=jnp.float32)
-    up_pre = jnp.dot(rows_in, up_w, preferred_element_type=jnp.float32)
-    sigmoid_gate = jax.nn.sigmoid(gate_pre)
-    active = gate_pre * sigmoid_gate
-    hidden = (active * up_pre).astype(jnp.bfloat16)
-    back_hidden = lax.dot_general(scaled, down_w, contract_last, preferred_element_type=jnp.float32)
-    grad_gate_pre = (
-        back_hidden * up_pre * sigmoid_gate * (1.0 + gate_pre * (1.0 - sigmoid_gate))
-    ).astype(jnp.bfloat16)
-    grad_up_pre = (back_hidden * active).astype(jnp.bfloat16)
-    score = jnp.sum(back_hidden * hidden.astype(jnp.float32), axis=1, keepdims=True)
-    score = jnp.broadcast_to(score, (row_total, LANES)).astype(jnp.bfloat16)
-    back = gather(grad_gate_pre, grad_up_pre, score, gate_w, up_w, expert_count, dp_count)
-    grad_down = lax.dot_general(
-        hidden, scaled, contract_first, preferred_element_type=jnp.float32
-    ).astype(jnp.bfloat16)
-    grad_gate = lax.dot_general(
-        rows_in, grad_gate_pre, contract_first, preferred_element_type=jnp.float32
-    ).astype(jnp.bfloat16)
-    grad_up = lax.dot_general(
-        rows_in, grad_up_pre, contract_first, preferred_element_type=jnp.float32
-    ).astype(jnp.bfloat16)
+    if row_total <= 1024 and (dp_count * capacity) % 16 == 0:
+        back, grad_gate, grad_up, grad_down = fused(
+            sent_in, sent_dy, w_gate[0].T, w_up[0].T, w_down[0], dp_count
+        )
+        grad_gate, grad_up = grad_gate.T, grad_up.T
+    else:
+        all_in, all_dy = spread(sent_in, sent_dy, dp_count)
+        rows_in = all_in.reshape(row_total, width)
+        scaled = all_dy.reshape(row_total, width)
+        gate_w = w_gate[0]
+        up_w = w_up[0]
+        down_w = w_down[0]
+        contract_last = (((1,), (1,)), ((), ()))
+        gate_pre = jnp.dot(rows_in, gate_w, preferred_element_type=jnp.float32)
+        up_pre = jnp.dot(rows_in, up_w, preferred_element_type=jnp.float32)
+        sigmoid_gate = jax.nn.sigmoid(gate_pre)
+        active = gate_pre * sigmoid_gate
+        hidden = (active * up_pre).astype(jnp.bfloat16)
+        back_hidden = lax.dot_general(scaled, down_w, contract_last, preferred_element_type=jnp.float32)
+        grad_gate_pre = (
+            back_hidden * up_pre * sigmoid_gate * (1.0 + gate_pre * (1.0 - sigmoid_gate))
+        ).astype(jnp.bfloat16)
+        grad_up_pre = (back_hidden * active).astype(jnp.bfloat16)
+        score = jnp.sum(back_hidden * hidden.astype(jnp.float32), axis=1, keepdims=True)
+        score = jnp.broadcast_to(score, (row_total, LANES)).astype(jnp.bfloat16)
+        back = gather(grad_gate_pre, grad_up_pre, score, gate_w, up_w, expert_count, dp_count)
+        grad_down = lax.dot_general(
+            hidden, scaled, contract_first, preferred_element_type=jnp.float32
+        ).astype(jnp.bfloat16)
+        grad_gate = lax.dot_general(
+            rows_in, grad_gate_pre, contract_first, preferred_element_type=jnp.float32
+        ).astype(jnp.bfloat16)
+        grad_up = lax.dot_general(
+            rows_in, grad_up_pre, contract_first, preferred_element_type=jnp.float32
+        ).astype(jnp.bfloat16)
     back = back.reshape(slot_total, width + LANES)
     grad_tokens = lax.dot_general(
         collect, back[:, :width], contract_first, preferred_element_type=jnp.float32

time: 257 us -> 205 us (0.80)
  matrix products: 37.2 us -> 7.89 us
  Pallas kernels: 200 us -> 189 us
  local copies, waits for them, and re-layouts: 13.8 us -> 5.11 us
    dot_general x6 -> x0, matrix products: 28.2 us -> none  [the longest x1 6.15 us: body(): gate_pre = jnp.dot(rows_in, gate_w, preferred_element_type=jnp.float32)]
    pallas_call x2 -> x1, Pallas kernels: 200 us -> 189 us  [fused(): pl.pallas_call(functools.partial(fused_kernel, count), out_shape=(full, f...]
    dot_general x2 -> x0, local copies, waits for them, and re-layouts: 4.42 us -> none  [the longest x1 2.21 us: body(): lax.dot_general(scaled, down_w, contract_last, preferred_element_type=jnp...]
    unnamed x22 -> x15, local copies, waits for them, and re-layouts: 6.3 us -> 5.11 us
where the time goes in v2:
time: 205 us; the launch traced here: 204 us
  Pallas kernels  189 us (92%)
  matrix products  7.89 us (4%)
  local copies, waits for them, and re-layouts  5.11 us (2%)
    pallas_call x1, Pallas kernels, fused(): pl.pallas_call(functools.partial(fused_kernel, count), out_shape=(full, f...  189 us
    unnamed x15, local copies, waits for them, and re-layouts  5.11 us

profile of v2, /device:TPU:11, one launch (start us, length us, event | category | flops | bytes accessed | tf_op | source)
XLA Modules:
  0.0 204.3 jit_solution(10572472643507745917)
XLA Ops:
  0.6 0.0 copy-start
  0.6 0.0 copy-start.5
  0.7 0.0 copy-start.4
  0.7 1.0 convert_reduce_fusion
  1.7 0.7 multiply_add_fusion
  2.3 0.0 copy-done
  2.3 1.7 convolution_convert_fusion.1
  4.0 0.0 copy-done.5
  4.0 0.0 copy-done.4
  4.0 1.7 convolution_convert_fusion
  5.7 189.0 %fused.1 = (bf16[4,8,24,4096]{3,2,1,0:T(8,128)(2,1)}, bf16[4,8,24,4096]{3,2,1,0:T(8,128)(2,1)}, bf16[8,24,4224]{2,1,0:T(8,128)(2,1)}, bf16[192,4096]{1,0:T(8,128...) custom-call(bf16[8,24,4096]{2,1,0:T(8,128)(2,1)} %bitcast.24, bf16[8,24,4096]{2,1,0:T(8,128)(2,1)} %bitcast.25, ...), custom_call_target="tpu_custom_call" | custom-call | tf_op jit(solution)/shard_map/fused/pallas_call | solution.py:611
  194.7 0.0 copy-start.3
  194.7 1.6 fusion.1
  196.3 2.9 %convolution_convert_fusion.2 = bf16[128,4096]{1,0:T(8,128)(2,1)} fusion(bf16[192,4224]{1,0:T(8,128)(2,1)} %bitcast.33, s32[128]{0:T(128)S(1)} %multiply_add_fusion), kind=kOutput, calls=%fused_computation.2 | convolution fusion | flops 201875456 | bytes 2621952 | tf_op jit(solution)/shard_map/dot_general | solution.py:722
  199.2 0.0 copy-done.3
  199.2 0.0 copy-start.2
  199.2 1.1 copy.15
  200.4 0.8 copy-done.2
  201.2 0.0 copy-start.1
  201.2 1.1 copy.16
  202.3 0.8 copy-done.1
  203.2 1.1 copy.17
Async XLA Ops:
  0.6 1.7 copy-start
  0.6 3.4 %copy-start.5 = (bf16[128,1]{0,1:T(2,128)(2,1)S(1)}, bf16[128,1]{0,1:T(2,128)(2,1)}, u32[]{:S(2)}) copy-start(bf16[128,1]{0,1:T(2,128)(2,1)} %param.10) | copy-start | bytes 772
  0.7 3.4 %copy-start.4 = (bf16[128,4096]{1,0:T(8,128)(2,1)S(1)}, bf16[128,4096]{1,0:T(8,128)(2,1)}, u32[]{:S(2)}) copy-start(bf16[128,4096]{1,0:T(8,128)(2,1)} %param.8) | copy-start | bytes 3145732
  194.7 4.5 %copy-start.3 = (bf16[192,4096]{1,0:T(8,128)(2,1)S(1)}, bf16[192,4096]{1,0:T(8,128)(2,1)}, u32[]{:S(2)}) copy-start(bf16[192,4096]{1,0:T(8,128)(2,1)} %get-tuple-element.10) | copy-start | bytes 4718596
  199.2 2.0 copy-start.2
  201.2 2.0 copy-start.1

commit v3 on v2

--- a/solution.py
+++ b/solution.py
@@ -362,7 +362,7 @@
 def fused_kernel(
     count, sent_in, sent_dy, gate_w, up_w, down_w,
     all_in, all_dy, back, grad_gate, grad_up, grad_down,
-    stage, flat_in, flat_dy, hid, dgate, dup, part, far_l, far_r, near_l, near_r, zed,
+    stage, flat_in, flat_dy, hid, dgate, dup, part, far_l, far_r, near_l, near_r, zed, total,
     z_s, z_r, side_s, side_r, far_s, far_r_sem, own_sem, stage_sem,
     rf_s, rf_r, rd_s, rd_r, rs_s, rs_r, home_s, home_r,
 ):
@@ -518,9 +518,9 @@
             rf_copy(way, i).wait_recv()
             for at in col_tiles(*spans[way], tile):
                 there = slice(at.start - spans[way][0], at.stop - spans[way][0])
-                total = part[sides[way], i, :, at].astype(jnp.float32)
-                total = total + far_in[way][i, :, there].astype(jnp.float32)
-                part[sides[way], i, :, at] = total.astype(part.dtype)
+                summed = part[sides[way], i, :, at].astype(jnp.float32)
+                summed = summed + far_in[way][i, :, there].astype(jnp.float32)
+                part[sides[way], i, :, at] = summed.astype(part.dtype)
             rs_copy(way, i).start()
 
     def merge(i):
@@ -528,22 +528,37 @@
             rd_copy(way, i).wait_recv()
             rs_copy(way, i).wait_recv()
         for at in col_tiles(0, cols, tile):
-            total = part[own_d, i, :, at].astype(jnp.float32)
-            total = total + near_l[i, :, at].astype(jnp.float32)
-            total = total + near_r[i, :, at].astype(jnp.float32)
-            zed[i, :, at] = total.astype(zed.dtype)
+            summed = part[own_d, i, :, at].astype(jnp.float32)
+            summed = summed + near_l[i, :, at].astype(jnp.float32)
+            summed = summed + near_r[i, :, at].astype(jnp.float32)
+            zed[i, :, at] = summed.astype(zed.dtype)
 
         @pl.when(i > 0)
         def _():
             home_copy(i).start()
 
-    def weight_grad(out, left_rows, right_rows):
+    def weight_grad(k, out, left_rows, right_rows, pair):
+        rows = pl.ds(pl.multiple_of(pair * 2 * group, 2 * group), 2 * group)
+        left_part = left_rows[rows, :]
+
         def one(j, carry):
             at = pl.ds(pl.multiple_of(j * tile, tile), tile)
             value = lax.dot_general(
-                left_rows[...], right_rows[:, at], first_dims, preferred_element_type=jnp.float32
+                left_part, right_rows[rows, at], first_dims, preferred_element_type=jnp.float32
             )
-            out[:, at] = value.astype(out.dtype)
+
+            @pl.when(pair == 0)
+            def _():
+                total[k, :, at] = value
+
+            @pl.when((pair > 0) & (pair < count // 2 - 1))
+            def _():
+                total[k, :, at] += value
+
+            @pl.when(pair == count // 2 - 1)
+            def _():
+                out[:, at] = (total[k, :, at] + value).astype(out.dtype)
+
             return carry
 
         lax.fori_loop(0, width // tile, one, 0)
@@ -561,10 +576,11 @@
         during(3, 0, ring_sum)
         during(2, 0, compute)
         during(4, 0, merge)
-        for k, grad in enumerate(grads):
-            @pl.when(t == count + 2 + (k + 1) // 2)
-            def _():
-                weight_grad(*grad)
+
+        @pl.when((t >= 4) & (t < count + 4) & (t % 2 == 0))
+        def _():
+            for k, grad in enumerate(grads):
+                weight_grad(k, *grad, (t - 4) // 2)
 
         return carry
 
@@ -601,7 +617,7 @@
     kind = sent_in.dtype
     hidden = down_w.shape[0]
     cols, half = width + LANES, width // 2
-    total = dp_count * count * cap
+    row_count = dp_count * count * cap
     dma = pltpu.SemaphoreType.DMA
     full = jax.ShapeDtypeStruct((dp_count, count, cap, width), kind)
     grad = jax.ShapeDtypeStruct((hidden, width), kind)
@@ -615,17 +631,18 @@
         out_specs=[apart, apart, apart, whole, whole, whole],
         scratch_shapes=[
             pltpu.VMEM((2, dp_count, cap, width), kind),
-            pltpu.VMEM((total, width), kind),
-            pltpu.VMEM((total, width), kind),
-            pltpu.VMEM((total, hidden), kind),
-            pltpu.VMEM((total, hidden), kind),
-            pltpu.VMEM((total, hidden), kind),
+            pltpu.VMEM((row_count, width), kind),
+            pltpu.VMEM((row_count, width), kind),
+            pltpu.VMEM((row_count, hidden), kind),
+            pltpu.VMEM((row_count, hidden), kind),
+            pltpu.VMEM((row_count, hidden), kind),
             pltpu.VMEM((dp_count, count, cap, cols), kind),
             pltpu.VMEM((count, cap, half), kind),
             pltpu.VMEM((count, cap, cols - half), kind),
             pltpu.VMEM((count, cap, cols), kind),
             pltpu.VMEM((count, cap, cols), kind),
             pltpu.VMEM((count, cap, cols), kind),
+            pltpu.VMEM((3, hidden, width), jnp.float32),
             pair,
             pair,
             dma((2, 2, count)),
@@ -683,7 +700,7 @@
     )
     contract_first = (((0,), (0,)), ((), ()))
     row_total = dp_count * slot_total
-    if row_total <= 1024 and (dp_count * capacity) % 16 == 0:
+    if row_total <= 1024 and expert_count % 2 == 0 and (dp_count * capacity) % 16 == 0:
         back, grad_gate, grad_up, grad_down = fused(
             sent_in, sent_dy, w_gate[0].T, w_up[0].T, w_down[0], dp_count
         )

time: 205 us -> 205 us (level)
  no operation moved by 1% of the time
where the time goes in v3:
time: 205 us
  Pallas kernels  189 us (92%)
  matrix products  7.88 us (4%)
  local copies, waits for them, and re-layouts  5.11 us (2%)
    pallas_call x1, Pallas kernels, fused(): pl.pallas_call(functools.partial(fused_kernel, count), out_shape=(full, f...  189 us
    unnamed x15, local copies, waits for them, and re-layouts  5.11 us

profile of v3, /device:TPU:11, one launch (start us, length us, event | category | flops | bytes accessed | tf_op | source)
XLA Modules:
  0.0 204.6 jit_solution(5662089220647519613)
XLA Ops:
  0.6 0.0 copy-start
  0.6 0.0 copy-start.5
  0.7 0.0 copy-start.4
  0.7 1.0 convert_reduce_fusion
  1.7 0.7 multiply_add_fusion
  2.3 0.0 copy-done
  2.3 1.7 convolution_convert_fusion.1
  4.0 0.0 copy-done.5
  4.0 0.0 copy-done.4
  4.0 1.7 convolution_convert_fusion
  5.7 189.2 %fused.1 = (bf16[4,8,24,4096]{3,2,1,0:T(8,128)(2,1)}, bf16[4,8,24,4096]{3,2,1,0:T(8,128)(2,1)}, bf16[8,24,4224]{2,1,0:T(8,128)(2,1)}, bf16[192,4096]{1,0:T(8,128...) custom-call(bf16[8,24,4096]{2,1,0:T(8,128)(2,1)} %bitcast.24, bf16[8,24,4096]{2,1,0:T(8,128)(2,1)} %bitcast.25, ...), custom_call_target="tpu_custom_call" | custom-call | tf_op jit(solution)/shard_map/fused/pallas_call | solution.py:627
  195.0 0.0 copy-start.3
  195.0 1.6 fusion.1
  196.6 2.9 %convolution_convert_fusion.2 = bf16[128,4096]{1,0:T(8,128)(2,1)} fusion(bf16[192,4224]{1,0:T(8,128)(2,1)} %bitcast.33, s32[128]{0:T(128)S(1)} %multiply_add_fusion), kind=kOutput, calls=%fused_computation.2 | convolution fusion | flops 201875456 | bytes 2621952 | tf_op jit(solution)/shard_map/dot_general | solution.py:739
  199.5 0.0 copy-done.3
  199.5 0.0 copy-start.2
  199.5 1.1 copy.15
  200.6 0.8 copy-done.2
  201.4 0.0 copy-start.1
  201.4 1.1 copy.16
  202.6 0.8 copy-done.1
  203.4 1.1 copy.17
Async XLA Ops:
  0.6 1.7 copy-start
  0.6 3.4 %copy-start.5 = (bf16[128,1]{0,1:T(2,128)(2,1)S(1)}, bf16[128,1]{0,1:T(2,128)(2,1)}, u32[]{:S(2)}) copy-start(bf16[128,1]{0,1:T(2,128)(2,1)} %param.10) | copy-start | bytes 772
  0.7 3.4 %copy-start.4 = (bf16[128,4096]{1,0:T(8,128)(2,1)S(1)}, bf16[128,4096]{1,0:T(8,128)(2,1)}, u32[]{:S(2)}) copy-start(bf16[128,4096]{1,0:T(8,128)(2,1)} %param.8) | copy-start | bytes 3145732
  195.0 4.5 %copy-start.3 = (bf16[192,4096]{1,0:T(8,128)(2,1)S(1)}, bf16[192,4096]{1,0:T(8,128)(2,1)}, u32[]{:S(2)}) copy-start(bf16[192,4096]{1,0:T(8,128)(2,1)} %get-tuple-element.10) | copy-start | bytes 4718596
  199.5 2.0 copy-start.2
  201.4 2.0 copy-start.1

commit v4 on v3

--- a/solution.py
+++ b/solution.py
@@ -451,7 +451,7 @@
             z_copy(a, i).start()
         return carry
 
-    lax.fori_loop(1, count, start, 0)
+    lax.fori_loop(1, min(4, count), start, 0)
     for a in range(2):
         own[a].wait()
 
@@ -460,6 +460,10 @@
             z_landed(a, i).wait_recv()
             for way in range(2):
                 side_copy(a, way, i).start()
+
+        @pl.when(i + 3 < count)
+        def _():
+            start(i + 3, 0)
 
     def onward(i):
         for a in range(2):

time: 205 us -> 205 us (level)
  no operation moved by 1% of the time
where the time goes in v4:
time: 205 us
  Pallas kernels  189 us (92%)
  matrix products  7.89 us (4%)
  local copies, waits for them, and re-layouts  5.11 us (2%)
    pallas_call x1, Pallas kernels, fused(): pl.pallas_call(functools.partial(fused_kernel, count), out_shape=(full, f...  189 us
    unnamed x15, local copies, waits for them, and re-layouts  5.11 us

profile of v4, /device:TPU:11, one launch (start us, length us, event | category | flops | bytes accessed | tf_op | source)
XLA Modules:
  0.0 204.6 jit_solution(4513500507260318546)
XLA Ops:
  0.6 0.0 copy-start
  0.6 0.0 copy-start.5
  0.7 0.0 copy-start.4
  0.7 1.0 convert_reduce_fusion
  1.7 0.7 multiply_add_fusion
  2.3 0.0 copy-done
  2.3 1.7 convolution_convert_fusion.1
  4.0 0.0 copy-done.5
  4.0 0.0 copy-done.4
  4.0 1.7 convolution_convert_fusion
  5.7 189.2 %fused.1 = (bf16[4,8,24,4096]{3,2,1,0:T(8,128)(2,1)}, bf16[4,8,24,4096]{3,2,1,0:T(8,128)(2,1)}, bf16[8,24,4224]{2,1,0:T(8,128)(2,1)}, bf16[192,4096]{1,0:T(8,128...) custom-call(bf16[8,24,4096]{2,1,0:T(8,128)(2,1)} %bitcast.24, bf16[8,24,4096]{2,1,0:T(8,128)(2,1)} %bitcast.25, ...), custom_call_target="tpu_custom_call" | custom-call | tf_op jit(solution)/shard_map/fused/pallas_call | solution.py:631
  195.0 0.0 copy-start.3
  195.0 1.6 fusion.1
  196.6 2.9 %convolution_convert_fusion.2 = bf16[128,4096]{1,0:T(8,128)(2,1)} fusion(bf16[192,4224]{1,0:T(8,128)(2,1)} %bitcast.33, s32[128]{0:T(128)S(1)} %multiply_add_fusion), kind=kOutput, calls=%fused_computation.2 | convolution fusion | flops 201875456 | bytes 2621952 | tf_op jit(solution)/shard_map/dot_general | solution.py:743
  199.5 0.0 copy-done.3
  199.5 0.0 copy-start.2
  199.5 1.1 copy.15
  200.6 0.8 copy-done.2
  201.5 0.0 copy-start.1
  201.5 1.1 copy.16
  202.6 0.8 copy-done.1
  203.4 1.1 copy.17
Async XLA Ops:
  0.6 1.7 copy-start
  0.6 3.4 %copy-start.5 = (bf16[128,1]{0,1:T(2,128)(2,1)S(1)}, bf16[128,1]{0,1:T(2,128)(2,1)}, u32[]{:S(2)}) copy-start(bf16[128,1]{0,1:T(2,128)(2,1)} %param.10) | copy-start | bytes 772
  0.7 3.4 %copy-start.4 = (bf16[128,4096]{1,0:T(8,128)(2,1)S(1)}, bf16[128,4096]{1,0:T(8,128)(2,1)}, u32[]{:S(2)}) copy-start(bf16[128,4096]{1,0:T(8,128)(2,1)} %param.8) | copy-start | bytes 3145732
  195.0 4.5 %copy-start.3 = (bf16[192,4096]{1,0:T(8,128)(2,1)S(1)}, bf16[192,4096]{1,0:T(8,128)(2,1)}, u32[]{:S(2)}) copy-start(bf16[192,4096]{1,0:T(8,128)(2,1)} %get-tuple-element.10) | copy-start | bytes 4718596
  199.5 2.0 copy-start.2
  201.5 2.0 copy-start.1
